TPU v7x, 32 devices: a whole 2x2x4 slice. The times are simulated.
32 devices in a mesh: groups: 2 (over y), pool: 4 (over z), head: 2 (over x), rep: 2 (over core).
Axes of the slice: x: 2, y: 2, z: 4, core: 2. Of those that a mesh axis runs over, the one named last changes fastest.
Arguments:
- queries: bfloat16 [2048, 4096], P(('groups', 'pool'), ('head', 'rep')), parts along dimension 0, may hold values from -200 to 200
- token_key_value: bfloat16 [2048, 1024], P(('groups', 'pool'), 'head'), parts along dimension 0, may hold values from -6 to 6
- key_value_cache: bfloat16 [96, 16, 1024], P(('groups', 'pool'), None, 'head'), parts along dimension 0, may hold values from -6 to 6
- cached_block_slots: int32 [24], P('groups'), parts along dimension 0, may hold values from 0 to 47, as said below
- absent_hidden_rows: bfloat16 [256, 8192], P(('groups', 'pool'), 'rep'), parts along dimension 0, may hold values from -6 to 6
- absent_block_count: int32 [8], P('groups'), parts along dimension 0, may hold values from 1 to 2, as said below
- adapter: int32 [2], P('groups'), parts along dimension 0, may hold values from 0 to 7
- key_value_weight: bfloat16 [8192, 1024], P('rep', 'head'), may hold values from -0.0625 to 0.0625
- down_weight_stack: bfloat16 [8, 16, 8192], P(None, None, 'rep'), may hold values from -0.0625 to 0.0625
- up_weight_stack: bfloat16 [8, 16, 1024], P(None, None, 'head'), may hold values from -0.75 to 0.75
Outputs:
- attended: bfloat16 [2048, 4096], P(('groups', 'pool'), ('head', 'rep')), parts along dimension 0
- rebuilt_key_value: bfloat16 [256, 1024], P(('groups', 'pool'), 'head'), parts along dimension 0
There are 2 independent parts, one for each index of `groups`. A program takes and returns all parts, laid end to end along the dimension named above; an argument that names none is the same for every part. Nothing has to cross between parts.
Inputs may be any that keep to these rules, and one draw needn't show every extreme that they name: `cached_block_slots`: entries are distinct cache slot numbers; slot s lies on pool device s // 12; no pool device holds more than 9 of the entries, and one holds exactly 9. `absent_block_count`: some pool device holds exactly 2 missing blocks.
All inputs are finite; a program needn't handle non-finite values.
Results may differ from a plain program's by a relative error of at most 0.011.
Values may be sent and summed in bfloat16 or wider, within the bound.
A program may use at most 64 MiB of HBM per device.

v0:
```python
import math

import jax
import jax.numpy as jnp
from jax import lax
from jax.sharding import PartitionSpec as P

HEAD_WIDTH = 128
KV_GROUP = 8
BLOCK = 16
OWNER_MOST = 9


ADAPTER_SCALE = 2.0
NEG_BIG = -1e30
block_limit = 512


def attend_block(state, query_rows, key_rows, value_rows, allowed):
    running_max, running_sum, weighted = state
    scores = jnp.einsum(
        "gmd,kgd->gmk", query_rows, key_rows, preferred_element_type=jnp.float32
    ) * HEAD_WIDTH ** (-0.5)
    scores = jnp.where(allowed[None], scores, NEG_BIG)
    new_max = jnp.maximum(running_max, jnp.max(scores, axis=-1))
    weights = jnp.where(allowed[None], jnp.exp(scores - new_max[..., None]), 0.0)
    rescale = jnp.exp(running_max - new_max)
    running_sum = running_sum * rescale + jnp.sum(weights, axis=-1)
    weighted = weighted * rescale[..., None] + jnp.einsum(
        "gmk,kgd->gmd", weights.astype(jnp.bfloat16), value_rows, preferred_element_type=jnp.float32
    )
    return (new_max, running_sum, weighted)


def attend_keys(state, query_rows, kv_rows, first_head, kv_groups, valid_fn):
    length = kv_rows.shape[0]
    head_count = kv_rows.shape[1] // (2 * HEAD_WIDTH)
    four_way = kv_rows.reshape(length, head_count, 2, HEAD_WIDTH)
    four_way = lax.dynamic_slice_in_dim(four_way, first_head, kv_groups, 1)
    block_len = math.gcd(length, block_limit)
    block_count = length // block_len
    if block_count == 1:
        positions = jnp.arange(length, dtype=jnp.int32)
        return attend_block(
            state, query_rows, four_way[:, :, 0], four_way[:, :, 1], valid_fn(positions)
        )
    split_rows = four_way.reshape(block_count, block_len, kv_groups, 2, HEAD_WIDTH)

    def one_block(inner_state, element):
        block_rows, offset = element
        positions = offset + jnp.arange(block_len, dtype=jnp.int32)
        return (
            attend_block(
                inner_state,
                query_rows,
                block_rows[:, :, 0],
                block_rows[:, :, 1],
                valid_fn(positions),
            ),
            None,
        )

    offsets = jnp.arange(block_count, dtype=jnp.int32) * block_len
    state, _ = lax.scan(one_block, state, (split_rows, offsets))
    return state


def shards(
    queries,
    token_key_value,
    key_value_cache,
    cached_block_slots,
    absent_hidden_rows,
    absent_block_count,
    adapter,
    key_value_weight,
    down_weight_stack,
    up_weight_stack,
):
    pool_size = lax.axis_size("pool")
    pool_index = lax.axis_index("pool")
    core_index = lax.axis_index("rep")
    tok_rows = queries.shape[0]
    heads_here = queries.shape[1] // HEAD_WIDTH
    kv_groups = max(1, heads_here // KV_GROUP)
    per_group = heads_here // kv_groups
    first_head = core_index * heads_here // KV_GROUP
    slot_count = key_value_cache.shape[0]
    owner_ids = jnp.arange(pool_size, dtype=jnp.int32)
    hit_owner = cached_block_slots // slot_count
    hit_count = jnp.sum((hit_owner[:, None] == owner_ids[None, :]).astype(jnp.int32), axis=0)
    owned = hit_owner == pool_index
    own_rank = jnp.cumsum(owned.astype(jnp.int32)) - 1
    picked = owned[None, :] & (
        own_rank[None, :] == jnp.arange(OWNER_MOST, dtype=jnp.int32)[:, None]
    )
    local_slot = jnp.sum(jnp.where(picked, (cached_block_slots % slot_count)[None, :], 0), axis=1)
    packed = jnp.take(key_value_cache, local_slot, axis=0).reshape(
        OWNER_MOST * BLOCK, key_value_cache.shape[2]
    )
    picked_down_weight = lax.dynamic_index_in_dim(down_weight_stack, adapter[0], 0, keepdims=False)
    picked_up_weight = lax.dynamic_index_in_dim(up_weight_stack, adapter[0], 0, keepdims=False)
    adapter_delta = jnp.einsum(
        "nd,rd->nr", absent_hidden_rows, picked_down_weight, preferred_element_type=jnp.float32
    )
    device_key_value = jnp.dot(
        absent_hidden_rows, key_value_weight, preferred_element_type=jnp.float32
    )
    device_key_value = device_key_value + ADAPTER_SCALE * jnp.dot(
        adapter_delta, picked_up_weight.astype(jnp.float32), precision=lax.Precision.HIGHEST
    )
    reduced_total = lax.psum(device_key_value, "rep")
    miss_rows = absent_hidden_rows.shape[0]
    miss_slots = miss_rows // BLOCK
    own_misses = jnp.sum(jnp.where(owner_ids == pool_index, absent_block_count, 0))
    present_rows = jnp.arange(miss_rows, dtype=jnp.int32) // BLOCK < own_misses
    rebuilt_key_value = jnp.where(present_rows[:, None], reduced_total, 0.0).astype(jnp.bfloat16)
    query_rows = (
        queries.reshape(tok_rows, kv_groups, per_group, HEAD_WIDTH)
        .transpose(1, 2, 0, 3)
        .reshape(kv_groups, per_group * tok_rows, HEAD_WIDTH)
    )
    query_pos = pool_index * tok_rows + jnp.arange(tok_rows, dtype=jnp.int32)

    def hit_valid(positions):
        block_ids = positions // BLOCK
        owners = block_ids // OWNER_MOST
        counts = jnp.sum(
            jnp.where(owners[:, None] == owner_ids[None, :], hit_count[None, :], 0), axis=1
        )
        return (block_ids % OWNER_MOST < counts)[None, :]

    def miss_valid(positions):
        block_ids = positions // BLOCK
        holders = block_ids // miss_slots
        counts = jnp.sum(
            jnp.where(holders[:, None] == owner_ids[None, :], absent_block_count[None, :], 0),
            axis=1,
        )
        return (block_ids % miss_slots < counts)[None, :]

    def span_valid(positions):
        return jnp.tile(positions[None, :] <= query_pos[:, None], (per_group, 1))

    state = (
        jnp.full((kv_groups, per_group * tok_rows), NEG_BIG, jnp.float32),
        jnp.zeros((kv_groups, per_group * tok_rows), jnp.float32),
        jnp.zeros((kv_groups, per_group * tok_rows, HEAD_WIDTH), jnp.float32),
    )
    state = attend_keys(
        state,
        query_rows,
        lax.all_gather(packed, "pool", axis=0, tiled=True),
        first_head,
        kv_groups,
        hit_valid,
    )
    state = attend_keys(
        state,
        query_rows,
        lax.all_gather(token_key_value, "pool", axis=0, tiled=True),
        first_head,
        kv_groups,
        span_valid,
    )
    state = attend_keys(
        state,
        query_rows,
        lax.all_gather(rebuilt_key_value, "pool", axis=0, tiled=True),
        first_head,
        kv_groups,
        miss_valid,
    )
    running_max, running_sum, weighted = state
    attended = (weighted / running_sum[..., None]).reshape(
        kv_groups, per_group, tok_rows, HEAD_WIDTH
    )
    attended = (
        attended.transpose(2, 0, 1, 3)
        .reshape(tok_rows, heads_here * HEAD_WIDTH)
        .astype(jnp.bfloat16)
    )
    return (attended, rebuilt_key_value)


def solution(mesh):
    in_specs = (
        P(("groups", "pool"), ("head", "rep")),
        P(("groups", "pool"), "head"),
        P(("groups", "pool"), None, "head"),
        P("groups"),
        P(("groups", "pool"), "rep"),
        P("groups"),
        P("groups"),
        P("rep", "head"),
        P(None, None, "rep"),
        P(None, None, "head"),
    )
    out_specs = (P(("groups", "pool"), ("head", "rep")), P(("groups", "pool"), "head"))
    return jax.shard_map(shards, mesh=mesh, in_specs=in_specs, out_specs=out_specs, check_vma=False)
```

profile of v0, /device:TPU:0, one launch (start us, length us, event | category | flops | bytes accessed | tf_op | source)
XLA Modules:
  0.0 130.1 jit_solution(9517576560635834270)
XLA Ops:
  7.2 1.9 %copy.35 = bf16[256,512]{0,1:T(8,128)(2,1)} copy(bf16[256,512]{1,0:T(8,128)(2,1)} %param.15) | data formatting | bytes 524288 | tf_op args[1]
  11.1 1.5 %gather_fusion = bf16[9,16,512]{2,1,0:T(8,128)(2,1)S(1)} fusion(bf16[12,16,512]{2,1,0:T(8,128)(2,1)} %param.16, s32[1024]{0:T(1024)S(1)} %pad_clamp_fusion), kind=kCustom, calls=%fused_computation | custom fusion | bytes 294948 | tf_op jit(solution)/shard_map/jit(_take)/gather | solution.py:98
  12.6 25.0 %all_gather.9 = bf16[576,512]{1,0:T(8,128)(2,1)S(1)} all-gather(bf16[144,512]{1,0:T(8,128)(2,1)S(1)} %bitcast_select_fusion.1), channel_id=1, replica_groups=mesh['groups'=2,'pool'=4,'head'=2,'rep'=2] {'pool'}, dimensions={0}, use_global_device_ids=true | all-gather | bytes 737280 | tf_op jit(solution)/shard_map/all_gather | solution.py:153
  37.9 1.1 copy.48
  40.1 37.4 %while.34 = (s32[]{:T(128)}, f32[1,2048]{1,0:T(1,128)S(1)}, f32[1,2048]{1,0:T(1,128)S(1)}, f32[1,2048,128]{2,1,0:T(8,128)S(1)}, s32[9]{0:T(128)S(1)}, /*index=5*...) while((s32[]{:T(128)}, f32[1,2048]{1,0:T(1,128)S(1)}, ...), condition=%wide.region_7.8_spmd.clone, body=%wide.region_3.7_spmd.clone.sunk | while | flops 69088896 | bytes 4491545 | solution.py:64
  43.3 1.0 fusion.85
  51.6 1.0 fusion.85
  59.9 1.0 fusion.85
  64.0 1.0 fusion.85
  68.2 1.0 fusion.85
  72.3 1.0 fusion.85
  78.2 3.0 %fusion.58 = f32[32,512]{1,0:T(8,128)S(1)} fusion(bf16[32,4096]{1,0:T(8,128)(2,1)S(1)} %copy-done.1, bf16[4096,512]{1,0:T(8,128)(2,1)} %param.21), kind=kOutput, calls=%fused_computation.130 | convolution fusion | flops 134217728 | bytes 4521984 | tf_op jit(solution)/shard_map/dot_general | solution.py:106
  82.3 3.6 %psum.7 = bf16[32,512]{1,0:T(8,128)(2,1)S(1)} all-reduce(f32[32,512]{1,0:T(8,128)S(1)} %fusion.36), channel_id=1, replica_groups=mesh['groups'=2,'pool'=4,'head'=2,'rep'=2] {'rep'}, use_global_device_ids=true, to_apply=%region_14.15 | all-reduce | flops 16384 | bytes 98304 | tf_op jit(solution)/shard_map/psum | solution.py:112
  87.3 13.3 %all_gather.11 = bf16[128,512]{1,0:T(8,128)(2,1)S(1)} all-gather(bf16[32,512]{1,0:T(8,128)(2,1)S(1)} %select_convert_fusion), channel_id=1, replica_groups=mesh['groups'=2,'pool'=4,'head'=2,'rep'=2] {'pool'}, dimensions={0}, use_global_device_ids=true | all-gather | bytes 163840 | tf_op jit(solution)/shard_map/all_gather | solution.py:169
  100.9 1.3 %fusion.57 = (f32[2048]{0:T(1024)S(1)}, f32[128,2048]{1,0:T(8,128)}) fusion(bf16[2048,128]{1,0:T(8,128)(2,1)S(1)} %bitcast.188, bf16[128,1,1,128]{3,2,1,0:T(2,128)(2,1)S(1)} %get-tuple-element.345, pred[128]{0:T(512)(128)(4,1)S(1)} %fusion.51), kind=kOutput, calls=%fused_computation.129 | convolution fusion | flops 67893248 | bytes 1613952 | tf_op jit(solution)/shard_map/gmd,kgd->gmk/dot_general | solution.py:21
  102.2 1.9 %constant_dynamic-slice_fusion.3 = bf16[1024,1,2,128]{0,3,2,1:T(8,128)(2,1)} fusion(bf16[1024,2,2,128]{0,3,2,1:T(8,128)(2,1)} %bitcast.206, s32[]{:T(128)S(6)} %select_n.204), kind=kLoop, calls=%fused_computation.107 | loop fusion | bytes 1048580 | tf_op jit(solution)/shard_map/dynamic_slice | solution.py:39
  104.1 1.3 %copy.36 = bf16[1024,1,2,128]{3,0,2,1:T(8,128)(2,1)S(1)} copy(bf16[1024,1,2,128]{0,3,2,1:T(8,128)(2,1)} %constant_dynamic-slice_fusion.3) | data formatting | bytes 1048576 | tf_op jit(solution)/shard_map/dynamic_slice | solution.py:39
  105.4 13.1 %while.33 = (s32[]{:T(128)}, f32[1,2048]{1,0:T(1,128)S(1)}, f32[1,2048]{1,0:T(1,128)S(1)}, f32[1,2048,128]{2,1,0:T(8,128)S(1)}, s32[2]{0:T(128)S(1)}, /*index=5*...) while((s32[]{:T(128)}, f32[1,2048]{1,0:T(1,128)S(1)}, ...), condition=%wide.region_11.12_spmd.clone, body=%wide.region_8.11_spmd.clone.sunk | while | flops 551162624 | bytes 22681716 | solution.py:64
  108.9 1.2 fusion.77
  110.2 1.7 %fusion.78 = f32[1,2048,128]{2,1,0:T(8,128)S(1)} fusion(pred[2048,512]{0,1:T(8,128)(4,1)S(1)} %bitcast.185, f32[512,2048]{1,0:T(8,128)S(1)} %get-tuple-element.447, f32[2048]{0:T(1024)S(1)} %bitcast.195, f32[1,2048,128]{2,1,0:T(8,128)S(1)} %get-tuple-element.504, f32[2048]{0:T(1024)S(1)} %bitcast.208, ...), kind=kOutput, calls=%fused_computation.9.clone.1 | convolution fusion | flops 274202624 | bytes 7487488 | tf_op jit(solution)/shard_map/while/body/eval_jaxpr/gmk,kgd->gmd/dot_general | solution.py:29
  115.4 1.2 fusion.77
  116.7 1.7 %fusion.78 = f32[1,2048,128]{2,1,0:T(8,128)S(1)} fusion(pred[2048,512]{0,1:T(8,128)(4,1)S(1)} %bitcast.185, f32[512,2048]{1,0:T(8,128)S(1)} %get-tuple-element.447, f32[2048]{0:T(1024)S(1)} %bitcast.195, f32[1,2048,128]{2,1,0:T(8,128)S(1)} %get-tuple-element.504, f32[2048]{0:T(1024)S(1)} %bitcast.208, ...), kind=kOutput, calls=%fused_computation.9.clone.1 | convolution fusion | flops 274202624 | bytes 7487488 | tf_op jit(solution)/shard_map/while/body/eval_jaxpr/gmk,kgd->gmd/dot_general | solution.py:29
  118.5 1.4 %fusion.37 = f32[2048]{0:T(1024)S(1)} fusion(f32[128,2048]{1,0:T(8,128)} %get-tuple-element.347, f32[2048]{0:T(1024)S(1)} %bitcast.209, pred[128]{0:T(512)(128)(4,1)S(1)} %fusion.51), kind=kLoop, calls=%fused_computation.68 | loop fusion | flops 784384 | bytes 1065088 | tf_op jit(solution)/shard_map/reduce_sum | solution.py:28
  120.0 2.1 %fusion.35 = bf16[1,2048,128]{2,1,0:T(8,128)(2,1)S(1)} fusion(f32[1,2048,128]{2,1,0:T(8,128)S(1)} %get-tuple-element.200, f32[128,2048]{1,0:T(8,128)} %get-tuple-element.347, f32[2048]{0:T(1024)S(1)} %bitcast.213, f32[2048]{0:T(1024)S(1)} %bitcast.210, f32[2048]{0:T(1024)S(1)} %bitcast.214, pred[128]{0:T(512)(128)(4,1)S(1)} %fusion.51, ...), kind=kOutput, calls=%fused_computation.64 | convolution fusion | flops 68943872 | bytes 2678912 | tf_op jit(solution)/shard_map/gmk,kgd->gmd/dot_general | solution.py:29
  (169 shorter events, 45.1 us)
Async XLA Ops:
  7.2 74.0 %copy-start = (bf16[8,16,4096]{2,1,0:T(8,128)(2,1)S(1)}, bf16[8,16,4096]{2,1,0:T(8,128)(2,1)}, u32[]{:S(2)}) copy-start(bf16[8,16,4096]{2,1,0:T(8,128)(2,1)} %param.22) | copy-start | bytes 3145732
  7.2 95.0 %all-gather.2.cloned.1.call-start = ((), (), s32[]{:S(2)}) async-start(), calls=%async_computation | async-start | bytes 1310720 | tf_op jit(solution)/shard_map/all_gather | solution.py:161
  40.1 38.0 %copy-start.1 = (bf16[32,4096]{1,0:T(8,128)(2,1)S(1)}, bf16[32,4096]{1,0:T(8,128)(2,1)}, u32[]{:S(2)}) copy-start(bf16[32,4096]{1,0:T(8,128)(2,1)} %param.18) | copy-start | bytes 786436
  77.5 8.5 %copy-start.3 = (s32[4]{0:T(128)S(1)}, s32[4]{0:T(128)}, u32[]{:S(2)}) copy-start(s32[4]{0:T(128)} %param.19) | copy-start | bytes 52
  87.3 18.1 %copy-start.2 = (bf16[32,512]{1,0:T(8,128)(2,1)}, bf16[32,512]{1,0:T(8,128)(2,1)S(1)}, u32[]{:S(2)}) copy-start(bf16[32,512]{1,0:T(8,128)(2,1)S(1)} %select_convert_fusion) | copy-start | bytes 98308
Sparse Core Ops, SparseCore 0:
  9.6 37.5 all-gather.1
where the time goes:
time: 131 us; the launch traced here: 130 us
  blocking collectives  42 us (32%)
  local copies, waits for them, and re-layouts  26.2 us (20%)
  matrix products  24.3 us (19%)
  other arithmetic  21.8 us (17%)
  between operations  14.9 us (11%)
    all_gather x1, blocking collectives, shards(): lax.all_gather(packed, 'pool', axis=0, tiled=True)  25 us
    dot_general x12, matrix products, attend_block(): jnp.einsum('gmk,kgd->gmd', weights.astype(jnp.bfloat16), value_rows, pref...  14.3 us
    dynamic_slice x29, local copies, waits for them, and re-layouts, attend_keys(): state, _ = lax.scan(one_block, state, (split_rows, offsets))  13.5 us
    all_gather x1, blocking collectives, shards(): lax.all_gather(rebuilt_key_value, 'pool', axis=0, tiled=True)  13.3 us
    dot_general x12, matrix products, attend_block(): jnp.einsum('gmd,kgd->gmk', query_rows, key_rows, preferred_element_type=j...  5.86 us
    lt x9, other arithmetic, hit_valid(): return (block_ids % OWNER_MOST < counts)[None, :]  5.22 us
    select_n x9, other arithmetic, hit_valid(): owners = block_ids // OWNER_MOST  5.18 us
    reduce_sum x12, other arithmetic, attend_block(): running_sum = running_sum * rescale + jnp.sum(weights, axis=-1)  5.03 us
  transfers between devices with their start and end apart: 1, of which 0 were waited for; matrix products, arithmetic and copies ran while one was open for 38% of the time, Pallas kernels for 0%

commit v1 on v0

v1 whole, which is shorter than its diff:
```python
import functools
import math

import jax
import jax.numpy as jnp
from jax import lax
from jax.experimental import pallas as pl
from jax.experimental.pallas import tpu as pltpu
from jax.sharding import PartitionSpec as P

HEAD_WIDTH = 128
KV_WIDTH = 2 * HEAD_WIDTH
KV_GROUP = 8
BLOCK = 16
OWNER_MOST = 9
ADAPTER_SCALE = 2.0
NEG_BIG = -1e30
MESH = pl.DeviceIdType.MESH
SCORE_SCALE = HEAD_WIDTH ** -0.5 * math.log2(math.e)
WEIGHT_CUTS = 4


def kernel(
    pool_size,
    slots_ref,
    count_ref,
    adapter_ref,
    query_hbm,
    token_hbm,
    cache_hbm,
    hidden_hbm,
    weight_hbm,
    down_hbm,
    up_hbm,
    out_ref,
    rebuilt_ref,
    query_ref,
    token_all,
    cache_ref,
    hidden_ref,
    weight_ref,
    down_ref,
    up_ref,
    hit_all,
    miss_all,
    part_send,
    part_recv,
    extra_kv,
    top_ref,
    acc_ref,
    local_sem,
    weight_sem,
    token_send,
    token_recv,
    hit_send,
    hit_recv,
    miss_send,
    miss_recv,
    part_sem,
):
    me = lax.axis_index("pool")
    core = lax.axis_index("rep")
    partner = 1 - core
    hits = slots_ref.shape[0]
    slot_count = cache_ref.shape[0]
    rows = query_ref.shape[0]
    heads = query_ref.shape[1] // HEAD_WIDTH
    first_head = core * heads // KV_GROUP
    columns = pl.ds(pl.multiple_of(first_head * KV_WIDTH, KV_WIDTH), KV_WIDTH)
    miss_rows = hidden_ref.shape[0]
    miss_slots = miss_rows // BLOCK

    barrier = pltpu.get_barrier_semaphore()
    for step in range(1, pool_size):
        pl.semaphore_signal(
            barrier, inc=1, device_id={"pool": lax.rem(me + step, pool_size)}, device_id_type=MESH
        )
    pl.semaphore_signal(barrier, inc=1, device_id={"rep": partner}, device_id_type=MESH)

    token_in = pltpu.make_async_copy(token_hbm.at[:, columns], token_all.at[me], local_sem.at[0])
    cache_in = pltpu.make_async_copy(cache_hbm.at[:, :, columns], cache_ref, local_sem.at[1])
    query_in = pltpu.make_async_copy(query_hbm, query_ref, local_sem.at[2])
    hidden_in = pltpu.make_async_copy(hidden_hbm, hidden_ref, local_sem.at[3])
    down_in = pltpu.make_async_copy(down_hbm, down_ref, local_sem.at[4])
    up_in = pltpu.make_async_copy(up_hbm, up_ref, local_sem.at[5])
    token_in.start()
    cache_in.start()
    query_in.start()
    hidden_in.start()
    depth = weight_ref.shape[0] // WEIGHT_CUTS
    weight_in = []
    for cut in range(WEIGHT_CUTS):
        span = pl.ds(cut * depth, depth)
        copy = pltpu.make_async_copy(weight_hbm.at[span], weight_ref.at[span], weight_sem.at[cut])
        copy.start()
        weight_in.append(copy)
    down_in.start()
    up_in.start()

    slot_ids = [slots_ref[i] for i in range(hits)]
    owners = [slot // slot_count for slot in slot_ids]
    ranks = []
    for i in range(hits):
        rank = jnp.int32(0)
        for j in range(i):
            rank = rank + (owners[j] == owners[i]).astype(jnp.int32)
        ranks.append(rank)
    place = [jnp.where(owners[i] == me, ranks[i], -1) for i in range(hits)]

    cache_in.wait()
    for j in range(OWNER_MOST):
        local_slot = jnp.int32(0)
        for i in range(hits):
            local_slot = jnp.where(place[i] == j, lax.rem(slot_ids[i], slot_count), local_slot)
        hit_all[me, j] = cache_ref[local_slot]
    token_in.wait()

    def remote(buffer, source, target, send, receive):
        return pltpu.make_async_remote_copy(
            src_ref=buffer.at[source],
            dst_ref=buffer.at[source],
            send_sem=send.at[target],
            recv_sem=receive.at[source],
            device_id={"pool": target},
            device_id_type=MESH,
        )

    pl.semaphore_wait(barrier, pool_size)
    for step in range(1, pool_size):

        @pl.when(me + step < pool_size)
        def _():
            remote(token_all, me, me + step, token_send, token_recv).start()

    for step in range(1, pool_size):
        target = lax.rem(me + step, pool_size)
        remote(hit_all, me, target, hit_send, hit_recv).start()

    def scores_of(head, keys):
        query = query_ref[:, head * HEAD_WIDTH : (head + 1) * HEAD_WIDTH]
        return (
            lax.dot_general(
                query, keys, (((1,), (1,)), ((), ())), preferred_element_type=jnp.float32
            )
            * SCORE_SCALE
        )

    def values_of(kv):
        return jnp.concatenate(
            [kv[:, HEAD_WIDTH:], jnp.ones((kv.shape[0], HEAD_WIDTH), kv.dtype)], axis=1
        )

    def first_attend(head_list):
        kv = token_all[me]
        keys, values = kv[:, :HEAD_WIDTH], values_of(kv)
        row_ids = lax.broadcasted_iota(jnp.int32, (rows, rows), 0)
        column_ids = lax.broadcasted_iota(jnp.int32, (rows, rows), 1)
        allowed = column_ids <= row_ids
        for head in head_list:
            score = jnp.where(allowed, scores_of(head, keys), NEG_BIG)
            top = jnp.max(score, axis=1, keepdims=True)
            weights = jnp.exp2(score - top).astype(jnp.bfloat16)
            top_ref[head] = jnp.broadcast_to(top, (rows, HEAD_WIDTH))
            acc_ref[head] = jnp.dot(weights, values, preferred_element_type=jnp.float32)

    def attend(kv, allowed, last):
        keys, values = kv[:, :HEAD_WIDTH], values_of(kv)
        for head in range(heads):
            score = scores_of(head, keys)
            if allowed is not None:
                score = jnp.where(allowed, score, NEG_BIG)
            old = top_ref[head][:, :1]
            top = jnp.maximum(old, jnp.max(score, axis=1, keepdims=True))
            weights = jnp.exp2(score - top).astype(jnp.bfloat16)
            total = acc_ref[head] * jnp.exp2(old - top) + jnp.dot(
                weights, values, preferred_element_type=jnp.float32
            )
            if last:
                out_ref[:, head * HEAD_WIDTH : (head + 1) * HEAD_WIDTH] = (
                    total[:, :HEAD_WIDTH] / total[:, HEAD_WIDTH:]
                ).astype(out_ref.dtype)
            else:
                top_ref[head] = jnp.broadcast_to(top, (rows, HEAD_WIDTH))
                acc_ref[head] = total

    query_in.wait()
    first_attend(range(heads // 2))

    hidden_in.wait()
    partial = None
    for cut in range(WEIGHT_CUTS):
        weight_in[cut].wait()
        span = slice(cut * depth, (cut + 1) * depth)
        product = jnp.dot(
            hidden_ref[:, span], weight_ref[span, :], preferred_element_type=jnp.float32
        )
        partial = product if partial is None else partial + product
    down_in.wait()
    up_in.wait()
    adapters, rank_width, width = down_ref.shape
    delta = lax.dot_general(
        hidden_ref[...],
        down_ref[...].reshape(adapters * rank_width, width),
        (((1,), (1,)), ((), ())),
        preferred_element_type=jnp.float32,
    )
    adapter_of = lax.broadcasted_iota(jnp.int32, delta.shape, 1) // rank_width
    delta = jnp.where(adapter_of == adapter_ref[0], delta, 0.0)
    up_all = up_ref[...].reshape(adapters * rank_width, up_ref.shape[2]).astype(jnp.float32)
    part_send[...] = partial + ADAPTER_SCALE * jnp.dot(
        delta, up_all, preferred_element_type=jnp.float32, precision=lax.Precision.HIGHEST
    )
    part_copy = pltpu.make_async_remote_copy(
        src_ref=part_send,
        dst_ref=part_recv,
        send_sem=part_sem.at[0],
        recv_sem=part_sem.at[1],
        device_id={"rep": partner},
        device_id_type=MESH,
    )
    part_copy.start()

    first_attend(range(heads // 2, heads))

    part_copy.wait_recv()
    present = lax.broadcasted_iota(jnp.int32, part_send.shape, 0) // BLOCK < count_ref[me]
    rebuilt_ref[...] = jnp.where(present, part_send[...] + part_recv[...], 0.0).astype(
        jnp.bfloat16
    )
    miss_all[me] = rebuilt_ref[:, columns]
    for step in range(1, pool_size):
        target = lax.rem(me + step, pool_size)
        remote(miss_all, me, target, miss_send, miss_recv).start()

    def earlier(step, carry):
        source = me - 1 - step
        remote(token_all, source, source, token_send, token_recv).wait_recv()
        attend(token_all[source], None, False)
        return carry

    lax.fori_loop(0, me, earlier, 0)

    for step in range(1, pool_size):
        source = lax.rem(me + step, pool_size)
        remote(hit_all, source, source, hit_send, hit_recv).wait_recv()
    for i in range(hits):
        extra_kv[i * BLOCK : (i + 1) * BLOCK, :] = hit_all[
            jnp.clip(owners[i], 0, pool_size - 1), jnp.minimum(ranks[i], OWNER_MOST - 1)
        ]
    for step in range(1, pool_size):
        source = lax.rem(me + step, pool_size)
        remote(miss_all, source, source, miss_send, miss_recv).wait_recv()
    for holder in range(pool_size):
        start = hits * BLOCK + holder * miss_rows
        extra_kv[start : start + miss_rows, :] = miss_all[holder]

    extra_rows = extra_kv.shape[0]
    ids = lax.broadcasted_iota(jnp.int32, (1, extra_rows), 1) - hits * BLOCK
    live = jnp.where(ids < 0, 1, 0)
    for holder in range(pool_size):
        offset = ids - holder * miss_rows
        limit = jnp.minimum(count_ref[holder], miss_slots) * BLOCK
        live = live + jnp.where((offset >= 0) & (offset < limit), 1, 0)
    attend(extra_kv[...], live > 0, True)

    for step in range(1, pool_size):

        @pl.when(me + step < pool_size)
        def _():
            remote(token_all, me, me + step, token_send, token_recv).wait_send()

    for step in range(1, pool_size):
        target = lax.rem(me + step, pool_size)
        remote(hit_all, me, target, hit_send, hit_recv).wait_send()
        remote(miss_all, me, target, miss_send, miss_recv).wait_send()
    part_copy.wait_send()


def shards(
    queries,
    token_key_value,
    key_value_cache,
    cached_block_slots,
    absent_hidden_rows,
    absent_block_count,
    adapter,
    key_value_weight,
    down_weight_stack,
    up_weight_stack,
):
    pool_size = lax.axis_size("pool")
    rows, query_width = queries.shape
    heads = query_width // HEAD_WIDTH
    slot_count = key_value_cache.shape[0]
    hits = cached_block_slots.shape[0]
    miss_rows = absent_hidden_rows.shape[0]
    kv_columns = token_key_value.shape[1]
    extra_rows = hits * BLOCK + pool_size * miss_rows
    smem = pl.BlockSpec(memory_space=pltpu.SMEM)
    anywhere = pl.BlockSpec(memory_space=pl.ANY)
    vmem = pl.BlockSpec(memory_space=pltpu.VMEM)
    dma = pltpu.SemaphoreType.DMA
    bf16 = jnp.bfloat16
    return pl.pallas_call(
        functools.partial(kernel, pool_size),
        out_shape=(
            jax.ShapeDtypeStruct((rows, query_width), bf16),
            jax.ShapeDtypeStruct((miss_rows, kv_columns), bf16),
        ),
        in_specs=[smem] * 3 + [anywhere] * 7,
        out_specs=(vmem, vmem),
        scratch_shapes=[
            pltpu.VMEM((rows, query_width), bf16),
            pltpu.VMEM((pool_size, rows, KV_WIDTH), bf16),
            pltpu.VMEM((slot_count, BLOCK, KV_WIDTH), bf16),
            pltpu.VMEM(absent_hidden_rows.shape, bf16),
            pltpu.VMEM(key_value_weight.shape, bf16),
            pltpu.VMEM(down_weight_stack.shape, bf16),
            pltpu.VMEM(up_weight_stack.shape, bf16),
            pltpu.VMEM((pool_size, OWNER_MOST, BLOCK, KV_WIDTH), bf16),
            pltpu.VMEM((pool_size, miss_rows, KV_WIDTH), bf16),
            pltpu.VMEM((miss_rows, kv_columns), jnp.float32),
            pltpu.VMEM((miss_rows, kv_columns), jnp.float32),
            pltpu.VMEM((extra_rows, KV_WIDTH), bf16),
            pltpu.VMEM((heads, rows, HEAD_WIDTH), jnp.float32),
            pltpu.VMEM((heads, rows, KV_WIDTH), jnp.float32),
            dma((6,)),
            dma((WEIGHT_CUTS,)),
            dma((pool_size,)),
            dma((pool_size,)),
            dma((pool_size,)),
            dma((pool_size,)),
            dma((pool_size,)),
            dma((pool_size,)),
            dma((2,)),
        ],
        compiler_params=pltpu.CompilerParams(
            collective_id=0, has_side_effects=True, vmem_limit_bytes=48 * 1024 * 1024
        ),
        cost_estimate=pl.CostEstimate(
            flops=4 * heads * rows * HEAD_WIDTH * (pool_size * rows + extra_rows),
            bytes_accessed=key_value_weight.size * 2,
            transcendentals=heads * rows * (pool_size * rows + extra_rows),
        ),
    )(
        cached_block_slots,
        absent_block_count,
        adapter,
        queries,
        token_key_value,
        key_value_cache,
        absent_hidden_rows,
        key_value_weight,
        down_weight_stack,
        up_weight_stack,
    )


def solution(mesh):
    in_specs = (
        P(("groups", "pool"), ("head", "rep")),
        P(("groups", "pool"), "head"),
        P(("groups", "pool"), None, "head"),
        P("groups"),
        P(("groups", "pool"), "rep"),
        P("groups"),
        P("groups"),
        P("rep", "head"),
        P(None, None, "rep"),
        P(None, None, "head"),
    )
    out_specs = (P(("groups", "pool"), ("head", "rep")), P(("groups", "pool"), "head"))
    return jax.shard_map(shards, mesh=mesh, in_specs=in_specs, out_specs=out_specs, check_vma=False)
```

time: 131 us -> 38.7 us (0.30)
  the two profiles are of different devices: /device:TPU:0 before, /device:TPU:26 now
where the time goes in v1:
time: 38.7 us; the launch traced here: 38.4 us
  Pallas kernels  28.4 us (73%)
  local copies, waits for them, and re-layouts  8.71 us (23%)
  between operations  1.3 us (3%)
    pallas_call x1, Pallas kernels, shards(): pl.pallas_call(functools.partial(kernel, pool_size), out_shape=(jax.Shape...  28.4 us
    unnamed x18, local copies, waits for them, and re-layouts  8.71 us

profile of v1, /device:TPU:26, one launch (start us, length us, event | category | flops | bytes accessed | tf_op | source)
XLA Modules:
  0.0 38.4 jit_solution(11229957151760462450)
XLA Ops:
  1.3 0.0 copy-start
  1.3 1.2 %copy-done = bf16[8,16,4096]{2,1,0:T(8,128)(2,1)S(1)} copy-done((bf16[8,16,4096]{2,1,0:T(8,128)(2,1)S(1)}, bf16[8,16,4096]{2,1,0:T(8,128)(2,1)}, u32[]{:S(2)}) %copy-start) | copy-done | bytes 1048600
  2.5 0.0 copy-start.1
  2.5 1.0 %copy-done.1 = bf16[256,1024]{1,0:T(8,128)(2,1)S(1)} copy-done((bf16[256,1024]{1,0:T(8,128)(2,1)S(1)}, bf16[256,1024]{1,0:T(8,128)(2,1)}, u32[]{:S(2)}) %copy-start.1) | copy-done | bytes 524312
  3.5 0.0 copy-start.2
  3.5 0.9 %copy-done.2 = bf16[256,512]{1,0:T(8,128)(2,1)S(1)} copy-done((bf16[256,512]{1,0:T(8,128)(2,1)S(1)}, bf16[256,512]{1,0:T(8,128)(2,1)}, u32[]{:S(2)}) %copy-start.2) | copy-done | bytes 262168
  4.5 0.0 copy-start.3
  4.5 0.9 %copy-done.3 = bf16[32,4096]{1,0:T(8,128)(2,1)S(1)} copy-done((bf16[32,4096]{1,0:T(8,128)(2,1)S(1)}, bf16[32,4096]{1,0:T(8,128)(2,1)}, u32[]{:S(2)}) %copy-start.3) | copy-done | bytes 262168
  5.4 0.0 copy-start.4
  5.4 0.9 %copy-done.4 = bf16[12,16,512]{2,1,0:T(8,128)(2,1)S(1)} copy-done((bf16[12,16,512]{2,1,0:T(8,128)(2,1)S(1)}, bf16[12,16,512]{2,1,0:T(8,128)(2,1)}, u32[]{:S(2)}) %copy-start.4) | copy-done | bytes 196632
  6.4 0.0 copy-start.5
  6.4 0.9 %copy-done.5 = bf16[8,16,512]{2,1,0:T(8,128)(2,1)S(1)} copy-done((bf16[8,16,512]{2,1,0:T(8,128)(2,1)S(1)}, bf16[8,16,512]{2,1,0:T(8,128)(2,1)}, u32[]{:S(2)}) %copy-start.5) | copy-done | bytes 131096
  7.3 0.0 copy-start.6
  7.3 0.7 %copy-done.6 = s32[12]{0:T(128)S(1)} copy-done((s32[12]{0:T(128)S(1)}, s32[12]{0:T(128)}, u32[]{:S(2)}) %copy-start.6) | copy-done | bytes 72
  7.9 0.0 copy-start.7
  7.9 0.7 %copy-done.7 = s32[4]{0:T(128)S(1)} copy-done((s32[4]{0:T(128)S(1)}, s32[4]{0:T(128)}, u32[]{:S(2)}) %copy-start.7) | copy-done | bytes 40
  8.6 28.4 %shard_map.113 = (bf16[256,1024]{1,0:T(8,128)(2,1)S(1)}, bf16[32,512]{1,0:T(8,128)(2,1)S(1)}) custom-call(s32[12]{0:T(128)S(1)} %copy-done.6, s32[4]{0:T(128)S(1)} %copy-done.7, s32[1]{0:T(128)S(6)} %copy.14.adapter_ref, bf16[256,1024]{1,0:T(8,128)(2,1)S(1)} %copy-done.1, bf16[256,512]{1,0:T(8,128)(2,1)S(1)} %copy-done.2, ...), custom_call_target="tpu_custom_call" | custom-call | flops 1409286144 | bytes 4194304 | tf_op jit(solution)/shard_map/pallas_call | solution.py:304
  37.0 0.8 %copy.15 = bf16[256,1024]{1,0:T(8,128)(2,1)} copy(bf16[256,1024]{1,0:T(8,128)(2,1)S(1)} %get-tuple-element.4) | data formatting | bytes 1048576
  37.8 0.6 %copy.16 = bf16[32,512]{1,0:T(8,128)(2,1)} copy(bf16[32,512]{1,0:T(8,128)(2,1)S(1)} %get-tuple-element.5) | data formatting | bytes 65536
Async XLA Ops:
  1.3 1.2 %copy-start = (bf16[8,16,4096]{2,1,0:T(8,128)(2,1)S(1)}, bf16[8,16,4096]{2,1,0:T(8,128)(2,1)}, u32[]{:S(2)}) copy-start(bf16[8,16,4096]{2,1,0:T(8,128)(2,1)} %down_hbm.1) | copy-start | bytes 3145732
  2.5 1.0 %copy-start.1 = (bf16[256,1024]{1,0:T(8,128)(2,1)S(1)}, bf16[256,1024]{1,0:T(8,128)(2,1)}, u32[]{:S(2)}) copy-start(bf16[256,1024]{1,0:T(8,128)(2,1)} %query_hbm.1) | copy-start | bytes 1572868
  3.5 0.9 %copy-start.2 = (bf16[256,512]{1,0:T(8,128)(2,1)S(1)}, bf16[256,512]{1,0:T(8,128)(2,1)}, u32[]{:S(2)}) copy-start(bf16[256,512]{1,0:T(8,128)(2,1)} %token_hbm.1) | copy-start | bytes 786436
  4.5 0.9 %copy-start.3 = (bf16[32,4096]{1,0:T(8,128)(2,1)S(1)}, bf16[32,4096]{1,0:T(8,128)(2,1)}, u32[]{:S(2)}) copy-start(bf16[32,4096]{1,0:T(8,128)(2,1)} %hidden_hbm.1) | copy-start | bytes 786436
  5.4 0.9 %copy-start.4 = (bf16[12,16,512]{2,1,0:T(8,128)(2,1)S(1)}, bf16[12,16,512]{2,1,0:T(8,128)(2,1)}, u32[]{:S(2)}) copy-start(bf16[12,16,512]{2,1,0:T(8,128)(2,1)} %cache_hbm.1) | copy-start | bytes 589828
  6.4 0.9 %copy-start.5 = (bf16[8,16,512]{2,1,0:T(8,128)(2,1)S(1)}, bf16[8,16,512]{2,1,0:T(8,128)(2,1)}, u32[]{:S(2)}) copy-start(bf16[8,16,512]{2,1,0:T(8,128)(2,1)} %up_hbm.1) | copy-start | bytes 393220
  7.3 0.7 %copy-start.6 = (s32[12]{0:T(128)S(1)}, s32[12]{0:T(128)}, u32[]{:S(2)}) copy-start(s32[12]{0:T(128)} %slots_ref.1) | copy-start | bytes 148
  7.9 0.7 %copy-start.7 = (s32[4]{0:T(128)S(1)}, s32[4]{0:T(128)}, u32[]{:S(2)}) copy-start(s32[4]{0:T(128)} %count_ref.1) | copy-start | bytes 52

commit v2 on v1

--- a/solution.py
+++ b/solution.py
@@ -126,11 +126,27 @@
         )
 
     pl.semaphore_wait(barrier, pool_size)
-    for step in range(1, pool_size):
-
-        @pl.when(me + step < pool_size)
+
+    def token_copy(source):
+        return pltpu.make_async_remote_copy(
+            src_ref=token_all.at[source],
+            dst_ref=token_all.at[source],
+            send_sem=token_send.at[source],
+            recv_sem=token_recv.at[source],
+            device_id={"pool": lax.rem(me + 1, pool_size)},
+            device_id_type=MESH,
+        )
+
+    def take_token(step):
+        token_copy(me - 1 - step).wait_recv()
+
+        @pl.when(me + 1 < pool_size)
         def _():
-            remote(token_all, me, me + step, token_send, token_recv).start()
+            token_copy(me - 1 - step).start()
+
+    @pl.when(me + 1 < pool_size)
+    def _():
+        token_copy(me).start()
 
     for step in range(1, pool_size):
         target = lax.rem(me + step, pool_size)
@@ -220,6 +236,10 @@
     )
     part_copy.start()
 
+    @pl.when(me > 0)
+    def _():
+        take_token(0)
+
     first_attend(range(heads // 2, heads))
 
     part_copy.wait_recv()
@@ -232,10 +252,16 @@
         target = lax.rem(me + step, pool_size)
         remote(miss_all, me, target, miss_send, miss_recv).start()
 
+    @pl.when(me > 1)
+    def _():
+        take_token(1)
+
     def earlier(step, carry):
-        source = me - 1 - step
-        remote(token_all, source, source, token_send, token_recv).wait_recv()
-        attend(token_all[source], None, False)
+        @pl.when(step > 1)
+        def _():
+            take_token(step)
+
+        attend(token_all[me - 1 - step], None, False)
         return carry
 
     lax.fori_loop(0, me, earlier, 0)
@@ -263,11 +289,11 @@
         live = live + jnp.where((offset >= 0) & (offset < limit), 1, 0)
     attend(extra_kv[...], live > 0, True)
 
-    for step in range(1, pool_size):
-
-        @pl.when(me + step < pool_size)
+    for source in range(pool_size):
+
+        @pl.when((source <= me) & (me + 1 < pool_size))
         def _():
-            remote(token_all, me, me + step, token_send, token_recv).wait_send()
+            token_copy(source).wait_send()
 
     for step in range(1, pool_size):
         target = lax.rem(me + step, pool_size)
@@ -335,7 +361,7 @@
             dma((2,)),
         ],
         compiler_params=pltpu.CompilerParams(
-            collective_id=0, has_side_effects=True, vmem_limit_bytes=48 * 1024 * 1024
+            collective_id=0, has_side_effects=True, vmem_limit_bytes=63 * 1024 * 1024
         ),
         cost_estimate=pl.CostEstimate(
             flops=4 * heads * rows * HEAD_WIDTH * (pool_size * rows + extra_rows),

time: 38.7 us -> 31.9 us (0.82)
  local copies, waits for them, and re-layouts: 8.71 us -> 3.24 us
  Pallas kernels: 28.4 us -> 27.1 us
    unnamed x18 -> x2, local copies, waits for them, and re-layouts: 8.71 us -> 3.24 us
    pallas_call x1, Pallas kernels: 28.4 us -> 27.1 us  [shards(): pl.pallas_call(functools.partial(kernel, pool_size), out_shape=(jax.Shape...]
where the time goes in v2:
time: 31.9 us; the launch traced here: 31.6 us
  Pallas kernels  27.1 us (85%)
  local copies, waits for them, and re-layouts  3.24 us (10%)
  between operations  1.29 us (4%)
    pallas_call x1, Pallas kernels, shards(): pl.pallas_call(functools.partial(kernel, pool_size), out_shape=(jax.Shape...  27.1 us
    unnamed x2, local copies, waits for them, and re-layouts  3.24 us

profile of v2, /device:TPU:26, one launch (start us, length us, event | category | flops | bytes accessed | tf_op | source)
XLA Modules:
  0.0 31.6 jit_solution(10614802180345118563)
XLA Ops:
  1.3 27.1 %shard_map.113 = (bf16[256,1024]{1,0:T(8,128)(2,1)}, bf16[32,512]{1,0:T(8,128)(2,1)}) custom-call(s32[12]{0:T(128)} %slots_ref.1, s32[4]{0:T(128)} %count_ref.1, s32[1]{0:T(128)S(6)} %copy.14.adapter_ref, bf16[256,1024]{1,0:T(8,128)(2,1)} %query_hbm.1, bf16[256,512]{1,0:T(8,128)(2,1)} %token_hbm.1, bf16[12,16,512]{2,1,0:T(8,128)(2,1)} %cache_hbm.1, ...), custom_call_target="tpu_custom_call" | custom-call | flops 1409286144 | bytes 4194304 | tf_op jit(solution)/shard_map/pallas_call | solution.py:330
  28.4 1.9 %copy.15 = bf16[256,1024]{1,0:T(8,128)(2,1)} copy(bf16[256,1024]{1,0:T(8,128)(2,1)} %get-tuple-element.4) | data formatting | bytes 1048576
  30.3 1.4 %copy.16 = bf16[32,512]{1,0:T(8,128)(2,1)} copy(bf16[32,512]{1,0:T(8,128)(2,1)} %get-tuple-element.5) | data formatting | bytes 65536

commit v3 on v2

--- a/solution.py
+++ b/solution.py
@@ -12,7 +12,6 @@
 KV_WIDTH = 2 * HEAD_WIDTH
 KV_GROUP = 8
 BLOCK = 16
-OWNER_MOST = 9
 ADAPTER_SCALE = 2.0
 NEG_BIG = -1e30
 MESH = pl.DeviceIdType.MESH
@@ -41,7 +40,10 @@
     weight_ref,
     down_ref,
     up_ref,
-    hit_all,
+    up_hits,
+    up_out,
+    down_hits,
+    down_out,
     miss_all,
     part_send,
     part_recv,
@@ -99,20 +101,59 @@
 
     slot_ids = [slots_ref[i] for i in range(hits)]
     owners = [slot // slot_count for slot in slot_ids]
-    ranks = []
+    cache_in.wait()
+
+    def own_block(i):
+        return cache_ref[lax.rem(slot_ids[i], slot_count)]
+
+    def up_copy():
+        return pltpu.make_async_remote_copy(
+            src_ref=up_out,
+            dst_ref=up_hits,
+            send_sem=hit_send.at[0],
+            recv_sem=hit_recv.at[0],
+            device_id={"pool": lax.rem(me + 1, pool_size)},
+            device_id_type=MESH,
+        )
+
+    def down_copy():
+        return pltpu.make_async_remote_copy(
+            src_ref=down_out,
+            dst_ref=down_hits,
+            send_sem=hit_send.at[1],
+            recv_sem=hit_recv.at[1],
+            device_id={"pool": lax.rem(me + pool_size - 1, pool_size)},
+            device_id_type=MESH,
+        )
+
+    def pass_hits(hop):
+        @pl.when(me == hop)
+        def _():
+            up_copy().wait_recv()
+            for i in range(hits):
+                up_out[i] = jnp.where(owners[i] == me, own_block(i), up_hits[i])
+            up_copy().start()
+
+        @pl.when(pool_size - 1 - me == hop)
+        def _():
+            down_copy().wait_recv()
+            for i in range(hits):
+                down_out[i] = jnp.where(owners[i] == me, own_block(i), down_hits[i])
+            down_copy().start()
+
     for i in range(hits):
-        rank = jnp.int32(0)
-        for j in range(i):
-            rank = rank + (owners[j] == owners[i]).astype(jnp.int32)
-        ranks.append(rank)
-    place = [jnp.where(owners[i] == me, ranks[i], -1) for i in range(hits)]
-
-    cache_in.wait()
-    for j in range(OWNER_MOST):
-        local_slot = jnp.int32(0)
+        extra_kv[i * BLOCK : (i + 1) * BLOCK, :] = own_block(i)
+
+    @pl.when(me == 0)
+    def _():
         for i in range(hits):
-            local_slot = jnp.where(place[i] == j, lax.rem(slot_ids[i], slot_count), local_slot)
-        hit_all[me, j] = cache_ref[local_slot]
+            up_out[i] = own_block(i)
+
+    @pl.when(me == pool_size - 1)
+    def _():
+        for i in range(hits):
+            down_out[i] = own_block(i)
+
     token_in.wait()
 
     def remote(buffer, source, target, send, receive):
@@ -148,9 +189,13 @@
     def _():
         token_copy(me).start()
 
-    for step in range(1, pool_size):
-        target = lax.rem(me + step, pool_size)
-        remote(hit_all, me, target, hit_send, hit_recv).start()
+    @pl.when(me == 0)
+    def _():
+        up_copy().start()
+
+    @pl.when(me == pool_size - 1)
+    def _():
+        down_copy().start()
 
     def scores_of(head, keys):
         query = query_ref[:, head * HEAD_WIDTH : (head + 1) * HEAD_WIDTH]
@@ -199,8 +244,15 @@
                 top_ref[head] = jnp.broadcast_to(top, (rows, HEAD_WIDTH))
                 acc_ref[head] = total
 
+    first_heads = heads * 3 // 4
     query_in.wait()
-    first_attend(range(heads // 2))
+    first_attend(range(first_heads))
+
+    @pl.when(me > 0)
+    def _():
+        take_token(0)
+
+    pass_hits(1)
 
     hidden_in.wait()
     partial = None
@@ -236,11 +288,12 @@
     )
     part_copy.start()
 
-    @pl.when(me > 0)
-    def _():
-        take_token(0)
-
-    first_attend(range(heads // 2, heads))
+    @pl.when(me > 1)
+    def _():
+        take_token(1)
+
+    pass_hits(2)
+    first_attend(range(first_heads, heads))
 
     part_copy.wait_recv()
     present = lax.broadcasted_iota(jnp.int32, part_send.shape, 0) // BLOCK < count_ref[me]
@@ -252,10 +305,6 @@
         target = lax.rem(me + step, pool_size)
         remote(miss_all, me, target, miss_send, miss_recv).start()
 
-    @pl.when(me > 1)
-    def _():
-        take_token(1)
-
     def earlier(step, carry):
         @pl.when(step > 1)
         def _():
@@ -266,13 +315,29 @@
 
     lax.fori_loop(0, me, earlier, 0)
 
-    for step in range(1, pool_size):
-        source = lax.rem(me + step, pool_size)
-        remote(hit_all, source, source, hit_send, hit_recv).wait_recv()
-    for i in range(hits):
-        extra_kv[i * BLOCK : (i + 1) * BLOCK, :] = hit_all[
-            jnp.clip(owners[i], 0, pool_size - 1), jnp.minimum(ranks[i], OWNER_MOST - 1)
-        ]
+    for hop in range(3, pool_size - 1):
+        pass_hits(hop)
+
+    @pl.when(me == pool_size - 1)
+    def _():
+        up_copy().wait_recv()
+
+    @pl.when(me == 0)
+    def _():
+        down_copy().wait_recv()
+
+    @pl.when(me > 0)
+    def _():
+        for i in range(hits):
+            span = slice(i * BLOCK, (i + 1) * BLOCK)
+            extra_kv[span, :] = jnp.where(owners[i] < me, up_hits[i], extra_kv[span, :])
+
+    @pl.when(me < pool_size - 1)
+    def _():
+        for i in range(hits):
+            span = slice(i * BLOCK, (i + 1) * BLOCK)
+            extra_kv[span, :] = jnp.where(owners[i] > me, down_hits[i], extra_kv[span, :])
+
     for step in range(1, pool_size):
         source = lax.rem(me + step, pool_size)
         remote(miss_all, source, source, miss_send, miss_recv).wait_recv()
@@ -297,9 +362,16 @@
 
     for step in range(1, pool_size):
         target = lax.rem(me + step, pool_size)
-        remote(hit_all, me, target, hit_send, hit_recv).wait_send()
         remote(miss_all, me, target, miss_send, miss_recv).wait_send()
     part_copy.wait_send()
+
+    @pl.when(me < pool_size - 1)
+    def _():
+        up_copy().wait_send()
+
+    @pl.when(me > 0)
+    def _():
+        down_copy().wait_send()
 
 
 def shards(
@@ -343,7 +415,10 @@
             pltpu.VMEM(key_value_weight.shape, bf16),
             pltpu.VMEM(down_weight_stack.shape, bf16),
             pltpu.VMEM(up_weight_stack.shape, bf16),
-            pltpu.VMEM((pool_size, OWNER_MOST, BLOCK, KV_WIDTH), bf16),
+            pltpu.VMEM((hits, BLOCK, KV_WIDTH), bf16),
+            pltpu.VMEM((hits, BLOCK, KV_WIDTH), bf16),
+            pltpu.VMEM((hits, BLOCK, KV_WIDTH), bf16),
+            pltpu.VMEM((hits, BLOCK, KV_WIDTH), bf16),
             pltpu.VMEM((pool_size, miss_rows, KV_WIDTH), bf16),
             pltpu.VMEM((miss_rows, kv_columns), jnp.float32),
             pltpu.VMEM((miss_rows, kv_columns), jnp.float32),
@@ -354,8 +429,8 @@
             dma((WEIGHT_CUTS,)),
             dma((pool_size,)),
             dma((pool_size,)),
-            dma((pool_size,)),
-            dma((pool_size,)),
+            dma((2,)),
+            dma((2,)),
             dma((pool_size,)),
             dma((pool_size,)),
             dma((2,)),

time: 31.9 us -> 29.6 us (0.928)
  the two profiles are of different devices: /device:TPU:26 before, /device:TPU:0 now
where the time goes in v3:
time: 29.6 us; the launch traced here: 29.4 us
  Pallas kernels  24.8 us (84%)
  local copies, waits for them, and re-layouts  3.24 us (11%)
  between operations  1.29 us (4%)
    pallas_call x1, Pallas kernels, shards(): pl.pallas_call(functools.partial(kernel, pool_size), out_shape=(jax.Shape...  24.8 us
    unnamed x2, local copies, waits for them, and re-layouts  3.24 us

profile of v3, /device:TPU:0, one launch (start us, length us, event | category | flops | bytes accessed | tf_op | source)
XLA Modules:
  0.0 29.4 jit_solution(14489666876960689039)
XLA Ops:
  1.3 24.8 %shard_map.113 = (bf16[256,1024]{1,0:T(8,128)(2,1)}, bf16[32,512]{1,0:T(8,128)(2,1)}) custom-call(s32[12]{0:T(128)} %slots_ref.1, s32[4]{0:T(128)} %count_ref.1, s32[1]{0:T(128)S(6)} %copy.14.adapter_ref, bf16[256,1024]{1,0:T(8,128)(2,1)} %query_hbm.1, bf16[256,512]{1,0:T(8,128)(2,1)} %token_hbm.1, bf16[12,16,512]{2,1,0:T(8,128)(2,1)} %cache_hbm.1, ...), custom_call_target="tpu_custom_call" | custom-call | flops 1409286144 | bytes 4194304 | tf_op jit(solution)/shard_map/pallas_call | solution.py:402
  26.1 1.9 %copy.15 = bf16[256,1024]{1,0:T(8,128)(2,1)} copy(bf16[256,1024]{1,0:T(8,128)(2,1)} %get-tuple-element.4) | data formatting | bytes 1048576
  28.0 1.4 %copy.16 = bf16[32,512]{1,0:T(8,128)(2,1)} copy(bf16[32,512]{1,0:T(8,128)(2,1)} %get-tuple-element.5) | data formatting | bytes 65536

commit v4 on v3

--- a/solution.py
+++ b/solution.py
@@ -246,13 +246,6 @@
 
     first_heads = heads * 3 // 4
     query_in.wait()
-    first_attend(range(first_heads))
-
-    @pl.when(me > 0)
-    def _():
-        take_token(0)
-
-    pass_hits(1)
 
     hidden_in.wait()
     partial = None
@@ -287,12 +280,7 @@
         device_id_type=MESH,
     )
     part_copy.start()
-
-    @pl.when(me > 1)
-    def _():
-        take_token(1)
-
-    pass_hits(2)
+    first_attend(range(first_heads))
     first_attend(range(first_heads, heads))
 
     part_copy.wait_recv()
@@ -304,6 +292,18 @@
     for step in range(1, pool_size):
         target = lax.rem(me + step, pool_size)
         remote(miss_all, me, target, miss_send, miss_recv).start()
+
+    @pl.when(me > 0)
+    def _():
+        take_token(0)
+
+    pass_hits(1)
+
+    @pl.when(me > 1)
+    def _():
+        take_token(1)
+
+    pass_hits(2)
 
     def earlier(step, carry):
         @pl.when(step > 1)

time: 29.6 us -> 28.1 us (0.949)
  the two profiles are of different devices: /device:TPU:0 before, /device:TPU:26 now
where the time goes in v4:
time: 28.1 us; the launch traced here: 27.6 us
  Pallas kernels  23.1 us (82%)
  local copies, waits for them, and re-layouts  3.24 us (12%)
  between operations  1.29 us (5%)
    pallas_call x1, Pallas kernels, shards(): pl.pallas_call(functools.partial(kernel, pool_size), out_shape=(jax.Shape...  23.1 us
    unnamed x2, local copies, waits for them, and re-layouts  3.24 us

profile of v4, /device:TPU:26, one launch (start us, length us, event | category | flops | bytes accessed | tf_op | source)
XLA Modules:
  0.0 27.6 jit_solution(7054338269122766389)
XLA Ops:
  1.3 23.1 %shard_map.113 = (bf16[256,1024]{1,0:T(8,128)(2,1)}, bf16[32,512]{1,0:T(8,128)(2,1)}) custom-call(s32[12]{0:T(128)} %slots_ref.1, s32[4]{0:T(128)} %count_ref.1, s32[1]{0:T(128)S(6)} %copy.14.adapter_ref, bf16[256,1024]{1,0:T(8,128)(2,1)} %query_hbm.1, bf16[256,512]{1,0:T(8,128)(2,1)} %token_hbm.1, bf16[12,16,512]{2,1,0:T(8,128)(2,1)} %cache_hbm.1, ...), custom_call_target="tpu_custom_call" | custom-call | flops 1409286144 | bytes 4194304 | tf_op jit(solution)/shard_map/pallas_call | solution.py:402
  24.4 1.9 %copy.15 = bf16[256,1024]{1,0:T(8,128)(2,1)} copy(bf16[256,1024]{1,0:T(8,128)(2,1)} %get-tuple-element.4) | data formatting | bytes 1048576
  26.3 1.4 %copy.16 = bf16[32,512]{1,0:T(8,128)(2,1)} copy(bf16[32,512]{1,0:T(8,128)(2,1)} %get-tuple-element.5) | data formatting | bytes 65536
